TPU v7x, 32 devices: a whole 2x2x4 slice. The times are simulated.
32 devices in a mesh: acq: 8 (over y, x, core), rcv: 4 (over z).
Axes of the slice: x: 2, y: 2, z: 4, core: 2. Of those that a mesh axis runs over, the one named last changes fastest.
Arguments:
- raw_blocks: bfloat16 [32, 1024, 512], P('acq', None, 'rcv'), may hold values from -6 to 6
- raw_dest: int32 [32], P('acq'), may hold values from 0 to 7, as said below
- raw_count: int32 [8], P('acq'), may hold values from 2 to 4, as said below
- stencil: int32 [512, 2], P('acq'), may hold values from 0 to 7, as said below
- stencil_weight: bfloat16 [512, 2], P('acq'), may hold values from 0.25 to 1
- kernel: bfloat16 [2, 2, 384], replicated, may hold values from -0.25 to 0.25
Outputs:
- multiples: bfloat16 [2, 512, 4, 2, 128], P(None, 'acq', 'rcv')
Inputs may be any that keep to these rules, and one draw needn't show every extreme that they name: `raw_dest`: within one group the 4 blocks go to different owners, so at most 1 to any owner, and every group reaches that; the first 2 blocks of group a go to the owners congruent to a modulo 4. `raw_count`: some group uses all 4 of its blocks. `stencil`: each row names two different slots of its owner's slot table that are filled by an in-use block.
All inputs are finite; a program needn't handle non-finite values.
Results may differ from a plain program's by a relative error of at most 0.0061.
Values may be sent and summed in bfloat16 or wider, within the bound.
A program may use at most 64 MiB of HBM per device.

v0:
```python
import math

import jax
import jax.numpy as jnp
from jax import lax
from jax.sharding import PartitionSpec as P

FLO = 32
CAP = 1


def passed_along(shard, axis, by):
    count = lax.axis_size(axis)
    return lax.ppermute(shard, axis, [(i, (i + by) % count) for i in range(count)])


def dft_table(freq_count, sample_count):
    freqs = FLO + jnp.arange(freq_count, dtype=jnp.int32)
    samples = jnp.arange(sample_count, dtype=jnp.int32)
    angles = (freqs[:, None] * samples[None, :] % sample_count).astype(jnp.float32) * (
        2.0 * math.pi / sample_count
    )
    cosines = jnp.stack([jnp.cos(angles), -jnp.sin(angles)], axis=1) / math.sqrt(sample_count)
    return cosines.reshape(2 * freq_count, sample_count).astype(jnp.bfloat16)


def block_operator(kernel, offset, stop_count, panel_width):
    shot_positions = (
        (offset + stop_count // 2) * panel_width
        + jnp.arange(panel_width, dtype=jnp.int32)[:, None]
        - jnp.arange(panel_width, dtype=jnp.int32)[None, :]
    )
    entries = jnp.take(kernel, shot_positions, axis=2)
    real_component = entries[:, 0]
    imag_part = entries[:, 1]
    upper_rows = jnp.concatenate([real_component, imag_part], axis=-1)
    lower_rows = jnp.concatenate([-imag_part, real_component], axis=-1)
    return jnp.concatenate([upper_rows, lower_rows], axis=1)


def accumulate(running_totals, receiver_panel, kernel, offset, stop_count, panel_width):
    prediction_operator = block_operator(kernel, offset, stop_count, panel_width)
    return running_totals + jnp.einsum(
        "pax,pxn->pan", receiver_panel, prediction_operator, preferred_element_type=jnp.float32
    )


def shards(raw_blocks, raw_dest, raw_count, stencil, stencil_weight, kernel):
    groups = lax.axis_size("acq")
    stop_count = lax.axis_size("rcv") // 2
    back_reach = stop_count // 2 - 1
    raw_slots, sample_count, panel_width = raw_blocks.shape
    slot_count = groups * CAP
    freq_count = kernel.shape[0]
    shot_rows = stencil.shape[0]
    fourier_rows = dft_table(freq_count, sample_count)
    block_index = jnp.arange(raw_slots, dtype=jnp.int32)
    slot_index = jnp.arange(slot_count, dtype=jnp.int32)
    is_live = block_index < raw_count[0]
    onehot = (
        (raw_dest[:, None] == jnp.arange(groups, dtype=jnp.int32)[None, :]) & is_live[:, None]
    ).astype(jnp.int32)
    slot_rank = jnp.sum(jnp.cumsum(onehot, axis=0) * onehot, axis=1) - 1
    slot_of = jnp.where(is_live, raw_dest * CAP + slot_rank, -1)
    select = (slot_of[None, :] == slot_index[:, None]).astype(jnp.bfloat16)
    spectra = jnp.einsum(
        "gt,rtp->rgp", fourier_rows, raw_blocks, preferred_element_type=jnp.float32
    ).astype(jnp.bfloat16)
    packed = jnp.dot(
        select, spectra.reshape(raw_slots, -1), preferred_element_type=jnp.float32
    ).astype(jnp.bfloat16)
    packed = packed.reshape(groups, CAP, 2 * freq_count * panel_width)
    received = lax.all_to_all(packed, "acq", split_axis=0, concat_axis=0, tiled=True)
    slot_rows = received.reshape(slot_count, freq_count, 2 * panel_width)
    weights = stencil_weight.astype(jnp.float32)
    mixing = jnp.where(stencil[:, 0, None] == slot_index[None, :], weights[:, 0, None], 0.0)
    mixing = mixing + jnp.where(
        stencil[:, 1, None] == slot_index[None, :], weights[:, 1, None], 0.0
    )
    mixing = mixing.astype(jnp.bfloat16)
    regular = jnp.einsum(
        "sq,qfx->fsx", mixing, slot_rows, preferred_element_type=jnp.float32
    ).astype(jnp.bfloat16)
    running_totals = jnp.zeros((freq_count, shot_rows, 2 * panel_width), jnp.float32)
    current = regular
    if back_reach > 0:
        current = passed_along(current, "rcv", back_reach)
    for stop_index in range(stop_count):
        if stop_index > 0:
            current = passed_along(current, "rcv", -1)
        running_totals = accumulate(
            running_totals, current, kernel, stop_index - back_reach, stop_count, panel_width
        )
    return running_totals.astype(jnp.bfloat16).reshape(freq_count, shot_rows, 1, 2, panel_width)


def solution(mesh):
    return jax.shard_map(
        shards,
        mesh=mesh,
        in_specs=(P("acq", None, "rcv"), P("acq"), P("acq"), P("acq", None), P("acq", None), P()),
        out_specs=P(None, "acq", "rcv", None, None),
        check_vma=False,
    )
```

profile of v0, /device:TPU:0, one launch (start us, length us, event | category | flops | bytes accessed | tf_op | source)
XLA Modules:
  0.0 254.7 jit_solution(6100568268196839471)
XLA Ops:
  0.8 0.7 fusion.40
  1.5 0.8 select_reduce_fusion
  2.4 0.3 fusion.30
  2.8 0.7 add_select_fusion
  3.4 0.2 fusion.2
  3.7 0.1 fusion.1
  3.8 0.5 broadcast.175
  4.3 0.6 reduce.1
  5.0 0.6 reshape.174
  5.6 5.2 %all-to-all-start = ((bf16[8,2,256]{2,1,0:T(2,128)(2,1)}), bf16[8,2,256]{2,1,0:T(2,128)(2,1)S(1)}, u32[]{:S(2)}, u32[]{:S(2)}) async-start(bf16[8,2,256]{2,1,0:T(2,128)(2,1)} %reshape.174), calls=%async_computation | async-start | bytes 16384 | tf_op jit(solution)/shard_map/all_to_all | solution.py:73
  10.8 0.1 bitcast_clamp_fusion.1
  10.9 0.1 fusion.22
  11.0 0.9 copy.30
  11.8 106.0 %gather_fusion = bf16[16384,2,2]{2,1,0:T(2,128)(2,1)} fusion(bf16[2,2,384]{1,0,2:T(2,128)(2,1)S(1)} %copy.30, s32[16384]{0:T(1024)S(1)} %bitcast_clamp_fusion.1), kind=kCustom, calls=%fused_computation.clone | custom fusion | bytes 327680 | tf_op jit(solution)/shard_map/jit(_take)/gather | solution.py:33
  117.8 11.9 %copy.35 = bf16[128,128,2,2]{1,0,2,3:T(8,128)(2,1)S(1)} copy(bf16[128,128,2,2]{3,2,1,0:T(2,128)(2,1)} %bitcast.53) | data formatting | bytes 262144 | tf_op jit(solution)/shard_map/jit(_take)/gather | solution.py:33
  129.9 0.1 fusion.23
  130.0 106.0 %gather_fusion.1 = bf16[16384,2,2]{2,1,0:T(2,128)(2,1)} fusion(bf16[2,2,384]{1,0,2:T(2,128)(2,1)S(1)} %copy.30, s32[16384]{0:T(1024)S(1)} %bitcast_clamp_fusion), kind=kCustom, calls=%fused_computation.1.clone | custom fusion | bytes 327680 | tf_op jit(solution)/shard_map/jit(_take)/gather | solution.py:33
  235.9 11.9 %copy.36 = bf16[128,128,2,2]{1,0,2,3:T(8,128)(2,1)S(1)} copy(bf16[128,128,2,2]{3,2,1,0:T(2,128)(2,1)} %bitcast.52) | data formatting | bytes 262144 | tf_op jit(solution)/shard_map/jit(_take)/gather | solution.py:33
  248.0 0.2 convolution_convert_fusion
  248.2 3.6 %collective-permute-start = (bf16[2,64,256]{2,1,0:T(8,128)(2,1)S(1)}, bf16[2,64,256]{2,1,0:T(8,128)(2,1)S(1)}, u32[]{:S(2)}, u32[]{:S(2)}) collective-permute-start(bf16[2,64,256]{2,1,0:T(8,128)(2,1)S(1)} %bitcast.54), channel_id=1, source_target_pairs={{0,3},{1,0},{2,1},{3,2},{4,7},{5,4},{6,5},{7,6},{8,11},{9,8},{10,9... | collective-permute-start | bytes 196616 | tf_op jit(solution)/shard_map/ppermute | solution.py:14
  251.9 0.2 fusion.3
  252.0 1.9 collective-permute-done
  253.9 0.2 fusion
  254.1 0.7 reshape.141
  (26 shorter events, 0.4 us)
Async XLA Ops:
  0.0 3.4 %copy-start = (bf16[4,1024,128]{2,1,0:T(8,128)(2,1)S(1)}, bf16[4,1024,128]{2,1,0:T(8,128)(2,1)}, u32[]{:S(2)}) copy-start(bf16[4,1024,128]{2,1,0:T(8,128)(2,1)} %param.8) | copy-start | bytes 3145732
  5.6 242.3 %all-to-all-start = ((bf16[8,2,256]{2,1,0:T(2,128)(2,1)}), bf16[8,2,256]{2,1,0:T(2,128)(2,1)S(1)}, u32[]{:S(2)}, u32[]{:S(2)}) async-start(bf16[8,2,256]{2,1,0:T(2,128)(2,1)} %reshape.174), calls=%async_computation | async-start | bytes 16384 | tf_op jit(solution)/shard_map/all_to_all | solution.py:73
  117.8 130.1 %copy-start.2 = (bf16[64,2]{0,1:T(2,128)(2,1)S(1)}, bf16[64,2]{0,1:T(2,128)(2,1)}, u32[]{:S(2)}) copy-start(bf16[64,2]{0,1:T(2,128)(2,1)} %param.12) | copy-start | bytes 772
  117.8 130.1 %copy-start.1 = (s32[64,2]{0,1:T(2,128)S(1)}, s32[64,2]{0,1:T(2,128)}, u32[]{:S(2)}) copy-start(s32[64,2]{0,1:T(2,128)} %param.11) | copy-start | bytes 1540
  248.2 5.7 %collective-permute-start = (bf16[2,64,256]{2,1,0:T(8,128)(2,1)S(1)}, bf16[2,64,256]{2,1,0:T(8,128)(2,1)S(1)}, u32[]{:S(2)}, u32[]{:S(2)}) collective-permute-start(bf16[2,64,256]{2,1,0:T(8,128)(2,1)S(1)} %bitcast.54), channel_id=1, source_target_pairs={{0,3},{1,0},{2,1},{3,2},{4,7},{5,4},{6,5},{7,6},{8,11},{9,8},{10,9... | collective-permute-start | bytes 196616 | tf_op jit(solution)/shard_map/ppermute | solution.py:14
where the time goes:
time: 255 us
  local copies, waits for them, and re-layouts  238 us (93%)
  starting transfers between devices  8.82 us (3%)
  other arithmetic  3.78 us (1%)
    gather x4, local copies, waits for them, and re-layouts, block_operator(): entries = jnp.take(kernel, shot_positions, axis=2)  236 us
    all_to_all x1, starting transfers between devices, shards(): lax.all_to_all(packed, 'acq', split_axis=0, concat_axis=0, tiled=True)  5.17 us
  transfers between devices with their start and end apart: 2, of which 1 were waited for; matrix products, arithmetic and copies ran while one was open for 93% of the time, Pallas kernels for 0%

commit v1 on v0

v1 whole, which is shorter than its diff:
```python
import functools
import math

import jax
import jax.numpy as jnp
import numpy as np
from jax import lax
from jax.experimental import pallas as pl
from jax.experimental.pallas import tpu as pltpu
from jax.sharding import PartitionSpec as P

FLO = 32
MESH = pl.DeviceIdType.MESH
F32 = jnp.float32
BF16 = jnp.bfloat16


def dft_table(freq_count, sample_count, row_count):
    freqs = FLO + np.arange(freq_count, dtype=np.int32)
    samples = np.arange(sample_count, dtype=np.int32)
    angles = (freqs[:, None] * samples[None, :] % sample_count).astype(np.float32) * np.float32(
        2.0 * math.pi / sample_count
    )
    rows = np.stack([np.cos(angles), -np.sin(angles)], axis=1) / np.float32(math.sqrt(sample_count))
    table = np.zeros((row_count, sample_count), np.float32)
    table[: 2 * freq_count] = rows.reshape(2 * freq_count, sample_count)
    return jnp.asarray(table, BF16)


def kernel(
    groups, panels, stops,
    table_hbm, raw_hbm, dest_hbm, count_hbm, stencil_hbm, weight_hbm, kern_hbm,
    out_ref,
    table, raw, dest, count, stencil, weight, kern, packed, received, slots, operator,
    raw_sems, small_sems, send_sem, recv_sems,
):
    raw_slots = raw.shape[0]
    rows = packed.shape[1]
    freq_count = rows // 2
    padded = slots.shape[0] // groups
    width = raw.shape[2]
    shot_count = stencil.shape[1]
    back_reach = stops // 2 - 1
    my_group = lax.axis_index("acq")
    my_panel = lax.axis_index("rcv")

    small = [
        pltpu.make_async_copy(src, dst, small_sems.at[at])
        for at, (src, dst) in enumerate([
            (table_hbm, table), (dest_hbm, dest), (count_hbm, count),
            (stencil_hbm, stencil), (weight_hbm, weight), (kern_hbm, kern),
        ])
    ]
    loads = [
        pltpu.make_async_copy(raw_hbm.at[j], raw.at[j], raw_sems.at[j]) for j in range(raw_slots)
    ]
    small[0].start()
    for load in loads:
        load.start()
    for copy in small[1:]:
        copy.start()

    def peers():
        for stop in range(stops):
            for step in range(groups):
                if stop != back_reach or step != 0:
                    yield stop, stop - back_reach, lax.rem(my_group + step, groups)

    barrier = pltpu.get_barrier_semaphore()
    for _, offset, group in peers():
        pl.semaphore_signal(
            barrier, inc=1,
            device_id={"acq": group, "rcv": lax.rem(my_panel + offset + panels, panels)},
            device_id_type=MESH,
        )

    small[0].wait()
    small[1].wait()
    small[2].wait()
    spectra = []
    for first in range(0, raw_slots, 2):
        blocks = list(range(first, min(first + 2, raw_slots)))
        for j in blocks:
            loads[j].wait()
        pair = jnp.concatenate([raw[j] for j in blocks], axis=1)
        both = jnp.dot(table[...], pair, preferred_element_type=F32)
        both = both.astype(BF16).astype(F32)
        for at in range(len(blocks)):
            spectra.append(both[:rows, at * width:(at + 1) * width])
    slot_of = [jnp.where(j < count[0], dest[j], -1) for j in range(raw_slots)]
    for owner in range(groups):
        total = jnp.zeros((rows, width), F32)
        for j in range(raw_slots):
            total = total + jnp.where(slot_of[j] == owner, 1.0, 0.0) * spectra[j]
        packed[owner] = total.astype(BF16)

    pl.semaphore_wait(barrier, groups * stops - 1)
    for stop, offset, group in peers():
        pltpu.make_async_remote_copy(
            src_ref=packed.at[group],
            dst_ref=received.at[stop, my_group],
            send_sem=send_sem,
            recv_sem=recv_sems.at[stop],
            device_id={"acq": group, "rcv": lax.rem(my_panel - offset + panels, panels)},
            device_id_type=MESH,
        ).start()
    received[back_reach, my_group] = packed[my_group]

    for copy in small[3:]:
        copy.wait()
    slots[...] = jnp.zeros_like(slots)
    lane = lax.broadcasted_iota(jnp.int32, (width, width), 1)
    row = lax.broadcasted_iota(jnp.int32, (width, width), 0)
    for f in range(freq_count):
        for c in range(2):
            line = kern[f, c:c + 1, :].astype(F32)
            if c == 1:
                line = -line
            rolled = [
                pltpu.roll(
                    jnp.broadcast_to(line[:, at * width:(at + 1) * width], (width, width)),
                    0, 1, stride=1, stride_axis=0,
                )
                for at in range(stops + 1)
            ]
            for stop in range(stops):
                place = (2 * stop + c) * width
                operator[f, :, place:place + width] = jnp.where(
                    lane >= row, rolled[stop + 1], rolled[stop]
                ).astype(BF16)

    slot_at = lax.broadcasted_iota(jnp.int32, (groups * padded, shot_count), 0) // padded
    weights = weight[...].astype(F32)
    mixing = jnp.where(slot_at == stencil[0:1, :], weights[0:1, :], 0.0)
    mixing = mixing + jnp.where(slot_at == stencil[1:2, :], weights[1:2, :], 0.0)
    spread_rows = lax.broadcasted_iota(jnp.int32, (2 * shot_count, shot_count), 0)
    spread_cols = lax.broadcasted_iota(jnp.int32, (2 * shot_count, shot_count), 1)
    spread = jnp.where(spread_rows // 2 == spread_cols, 1.0, 0.0).astype(BF16)
    mixing = lax.dot_general(
        spread, mixing.astype(BF16), (((1,), (1,)), ((), ())), preferred_element_type=F32
    )
    part = lax.broadcasted_iota(jnp.int32, mixing.shape, 0) % 2
    component = lax.broadcasted_iota(jnp.int32, mixing.shape, 1) % padded
    mixers = []
    for f in range(freq_count):
        mixers.append(jnp.where(component == 2 * f + part, mixing, 0.0).astype(BF16))
        signed = jnp.where(part == 0, mixing, -mixing)
        mixers.append(jnp.where(component == 2 * f + 1 - part, signed, 0.0).astype(BF16))
    mixers = jnp.concatenate(mixers, axis=0)

    for stop in range(stops):
        arrived = received.at[stop]
        if stop == back_reach:
            arrived = received.at[stop, pl.ds(0, groups - 1)]
        pltpu.make_async_copy(arrived, arrived, recv_sems.at[stop]).wait()
        for group in range(groups):
            slots[group * padded:group * padded + rows, stop * width:(stop + 1) * width] = (
                received[stop, group].astype(F32)
            )
    regular = jnp.dot(mixers, slots[...].astype(BF16), preferred_element_type=F32).astype(BF16)
    pairs = 2 * shot_count
    for f in range(freq_count):
        fields = []
        for stop in range(stops):
            for c in range(2):
                at = (2 * f + c) * pairs
                fields.append(regular[at:at + pairs, stop * width:(stop + 1) * width])
        fields = jnp.concatenate(fields, axis=1)
        out_ref[f] = lax.dot_general(
            fields, operator[f], (((1,), (1,)), ((), ())), preferred_element_type=F32
        ).astype(BF16)

    for stop in range(stops):
        sent = packed
        if stop == back_reach:
            sent = packed.at[pl.ds(0, groups - 1)]
        pltpu.make_async_copy(sent, sent, send_sem).wait()


def shards(raw_blocks, raw_dest, raw_count, stencil, stencil_weight, kern):
    groups = lax.axis_size("acq")
    panels = lax.axis_size("rcv")
    stops = panels // 2
    raw_slots, sample_count, width = raw_blocks.shape
    freq_count = kern.shape[0]
    shot_count = stencil.shape[0]
    rows = 2 * freq_count
    padded = -(-rows // 8) * 8
    table = dft_table(freq_count, sample_count, -(-rows // 16) * 16)
    out = pl.pallas_call(
        functools.partial(kernel, groups, panels, stops),
        out_shape=jax.ShapeDtypeStruct((freq_count, 2 * shot_count, width), BF16),
        in_specs=[pl.BlockSpec(memory_space=pl.ANY)] * 7,
        out_specs=pl.BlockSpec(memory_space=pltpu.VMEM),
        scratch_shapes=[
            pltpu.VMEM(table.shape, BF16),
            pltpu.VMEM(raw_blocks.shape, BF16),
            pltpu.SMEM(raw_dest.shape, jnp.int32),
            pltpu.SMEM(raw_count.shape, jnp.int32),
            pltpu.VMEM((2, shot_count), jnp.int32),
            pltpu.VMEM((2, shot_count), BF16),
            pltpu.VMEM(kern.shape, BF16),
            pltpu.VMEM((groups, rows, width), BF16),
            pltpu.VMEM((stops, groups, rows, width), BF16),
            pltpu.VMEM((groups * padded, stops * width), F32),
            pltpu.VMEM((freq_count, width, 2 * stops * width), BF16),
            pltpu.SemaphoreType.DMA((raw_slots,)),
            pltpu.SemaphoreType.DMA((6,)),
            pltpu.SemaphoreType.DMA,
            pltpu.SemaphoreType.DMA((stops,)),
        ],
        compiler_params=pltpu.CompilerParams(
            collective_id=0, has_side_effects=True, vmem_limit_bytes=60 * 1024 * 1024
        ),
    )(table, raw_blocks, raw_dest, raw_count, stencil.T, stencil_weight.T, kern)
    return out.reshape(freq_count, shot_count, 1, 2, width)


def solution(mesh):
    return jax.shard_map(
        shards,
        mesh=mesh,
        in_specs=(P("acq", None, "rcv"), P("acq"), P("acq"), P("acq", None), P("acq", None), P()),
        out_specs=P(None, "acq", "rcv", None, None),
        check_vma=False,
    )
```

time: 255 us -> 12.7 us (0.05)
  local copies, waits for them, and re-layouts: 238 us -> 1.52 us
  Pallas kernels: 0 us -> 10.3 us
  starting transfers between devices: 8.82 us -> 0 us
  other arithmetic: 3.78 us -> 0 us
    gather x4 -> x0, local copies, waits for them, and re-layouts: 236 us -> none  [block_operator(): entries = jnp.take(kernel, shot_positions, axis=2)]
    pallas_call x0 -> x1, Pallas kernels: none -> 10.3 us  [shards(): pl.pallas_call(functools.partial(kernel, groups, panels, stops), out_shap...]
    all_to_all x1 -> x0, starting transfers between devices: 5.17 us -> none  [shards(): lax.all_to_all(packed, 'acq', split_axis=0, concat_axis=0, tiled=True)]
    ppermute x1 -> x0, starting transfers between devices: 3.65 us -> none  [passed_along(): lax.ppermute(shard, axis, [(i, (i + by) % count) for i in range(count)])]
  transfers between devices with their start and end apart: 2 -> 0, of which waited for: 1 -> 0; matrix products, arithmetic and copies ran while one was open for 93% -> 0% of each run, Pallas kernels for 0% -> 0%
where the time goes in v1:
time: 12.7 us; the launch traced here: 12.5 us
  Pallas kernels  10.3 us (81%)
  local copies, waits for them, and re-layouts  1.52 us (12%)
  between operations  0.66 us (5%)
    pallas_call x1, Pallas kernels, shards(): pl.pallas_call(functools.partial(kernel, groups, panels, stops), out_shap...  10.3 us
    unnamed x1, local copies, waits for them, and re-layouts  1.52 us

profile of v1, /device:TPU:0, one launch (start us, length us, event | category | flops | bytes accessed | tf_op | source)
XLA Modules:
  0.0 12.5 jit_solution(16535965822188324259)
XLA Ops:
  0.7 10.3 %shard_map.73 = bf16[2,128,128]{2,1,0:T(8,128)(2,1)} custom-call(bf16[16,1024]{1,0:T(8,128)(2,1)} %constant.2.clone.table_hbm, bf16[4,1024,128]{2,1,0:T(8,128)(2,1)} %raw_hbm.1, s32[4]{0:T(128)} %dest_hbm.1, s32[1]{0:T(128)S(6)} %copy.10.count_hbm, s32[2,64]{1,0:T(2,128)} %bitcast.6, bf16[2,64]{1,0:T(2,128)(2,1)} %bitcast.7, bf16[2,2,384]{2,1,0:T(2,128)(2,1)} %kern_hbm.1), custom_call_target="tpu_custom_call" | custom-call | tf_op jit(solution)/shard_map/pallas_call | solution.py:190
  11.0 1.5 %copy.11 = bf16[2,64,1,2,128]{4,3,2,1,0:T(2,128)(2,1)} copy(bf16[2,64,1,2,128]{4,3,2,1,0:T(2,128)(2,1)} %bitcast.5) | data formatting | bytes 131072

commit v2 on v1

--- a/solution.py
+++ b/solution.py
@@ -37,7 +37,7 @@
     raw_slots = raw.shape[0]
     rows = packed.shape[1]
     freq_count = rows // 2
-    padded = slots.shape[0] // groups
+    padded = slots.shape[1] // groups
     width = raw.shape[2]
     shot_count = stencil.shape[1]
     back_reach = stops // 2 - 1
@@ -60,17 +60,25 @@
     for copy in small[1:]:
         copy.start()
 
+    def moved(place, by, count):
+        place = place + by
+        if by < 0:
+            return jnp.where(place < 0, place + count, place)
+        return jnp.where(place >= count, place - count, place)
+
+    far_first = sorted(range(stops), key=lambda stop: -abs(stop - back_reach))
+
     def peers():
-        for stop in range(stops):
+        for stop in far_first:
             for step in range(groups):
                 if stop != back_reach or step != 0:
-                    yield stop, stop - back_reach, lax.rem(my_group + step, groups)
+                    yield stop, stop - back_reach, moved(my_group, step, groups)
 
     barrier = pltpu.get_barrier_semaphore()
     for _, offset, group in peers():
         pl.semaphore_signal(
             barrier, inc=1,
-            device_id={"acq": group, "rcv": lax.rem(my_panel + offset + panels, panels)},
+            device_id={"acq": group, "rcv": moved(my_panel, offset, panels)},
             device_id_type=MESH,
         )
 
@@ -101,7 +109,7 @@
             dst_ref=received.at[stop, my_group],
             send_sem=send_sem,
             recv_sem=recv_sems.at[stop],
-            device_id={"acq": group, "rcv": lax.rem(my_panel - offset + panels, panels)},
+            device_id={"acq": group, "rcv": moved(my_panel, -offset, panels)},
             device_id_type=MESH,
         ).start()
     received[back_reach, my_group] = packed[my_group]
@@ -148,27 +156,29 @@
         mixers.append(jnp.where(component == 2 * f + 1 - part, signed, 0.0).astype(BF16))
     mixers = jnp.concatenate(mixers, axis=0)
 
-    for stop in range(stops):
+    pairs = 2 * shot_count
+    totals = [jnp.zeros((pairs, width), F32)] * freq_count
+    for stop in reversed(far_first):
         arrived = received.at[stop]
         if stop == back_reach:
             arrived = received.at[stop, pl.ds(0, groups - 1)]
         pltpu.make_async_copy(arrived, arrived, recv_sems.at[stop]).wait()
         for group in range(groups):
-            slots[group * padded:group * padded + rows, stop * width:(stop + 1) * width] = (
-                received[stop, group].astype(F32)
+            slots[stop, group * padded:group * padded + rows] = received[stop, group].astype(F32)
+        regular = jnp.dot(
+            mixers, slots[stop].astype(BF16), preferred_element_type=F32
+        ).astype(BF16)
+        for f in range(freq_count):
+            at = 2 * f * pairs
+            fields = jnp.concatenate(
+                [regular[at:at + pairs], regular[at + pairs:at + 2 * pairs]], axis=1
             )
-    regular = jnp.dot(mixers, slots[...].astype(BF16), preferred_element_type=F32).astype(BF16)
-    pairs = 2 * shot_count
+            totals[f] = totals[f] + lax.dot_general(
+                fields, operator[f, :, 2 * stop * width:2 * (stop + 1) * width],
+                (((1,), (1,)), ((), ())), preferred_element_type=F32,
+            )
     for f in range(freq_count):
-        fields = []
-        for stop in range(stops):
-            for c in range(2):
-                at = (2 * f + c) * pairs
-                fields.append(regular[at:at + pairs, stop * width:(stop + 1) * width])
-        fields = jnp.concatenate(fields, axis=1)
-        out_ref[f] = lax.dot_general(
-            fields, operator[f], (((1,), (1,)), ((), ())), preferred_element_type=F32
-        ).astype(BF16)
+        out_ref[f] = totals[f].astype(BF16)
 
     for stop in range(stops):
         sent = packed
@@ -187,10 +197,11 @@
     rows = 2 * freq_count
     padded = -(-rows // 8) * 8
     table = dft_table(freq_count, sample_count, -(-rows // 16) * 16)
+    args = (table, raw_blocks, raw_dest, raw_count, stencil.T, stencil_weight.T, kern)
     out = pl.pallas_call(
         functools.partial(kernel, groups, panels, stops),
-        out_shape=jax.ShapeDtypeStruct((freq_count, 2 * shot_count, width), BF16),
-        in_specs=[pl.BlockSpec(memory_space=pl.ANY)] * 7,
+        out_shape=pltpu.VMEM((freq_count, 2 * shot_count, width), BF16),
+        in_specs=[pl.BlockSpec(memory_space=pltpu.HBM)] * 7,
         out_specs=pl.BlockSpec(memory_space=pltpu.VMEM),
         scratch_shapes=[
             pltpu.VMEM(table.shape, BF16),
@@ -202,7 +213,7 @@
             pltpu.VMEM(kern.shape, BF16),
             pltpu.VMEM((groups, rows, width), BF16),
             pltpu.VMEM((stops, groups, rows, width), BF16),
-            pltpu.VMEM((groups * padded, stops * width), F32),
+            pltpu.VMEM((stops, groups * padded, width), F32),
             pltpu.VMEM((freq_count, width, 2 * stops * width), BF16),
             pltpu.SemaphoreType.DMA((raw_slots,)),
             pltpu.SemaphoreType.DMA((6,)),
@@ -210,9 +221,9 @@
             pltpu.SemaphoreType.DMA((stops,)),
         ],
         compiler_params=pltpu.CompilerParams(
-            collective_id=0, has_side_effects=True, vmem_limit_bytes=60 * 1024 * 1024
+            collective_id=0, has_side_effects=True, vmem_limit_bytes=32 * 1024 * 1024
         ),
-    )(table, raw_blocks, raw_dest, raw_count, stencil.T, stencil_weight.T, kern)
+    )(*(pltpu.with_memory_space_constraint(arg, pltpu.HBM) if arg.size > 1 else arg for arg in args))
     return out.reshape(freq_count, shot_count, 1, 2, width)
 
 

time: 12.7 us -> 11.3 us (0.89)
  local copies, waits for them, and re-layouts: 1.52 us -> 0.63 us
  Pallas kernels: 10.3 us -> 9.83 us
    unnamed x1, local copies, waits for them, and re-layouts: 1.52 us -> 0.63 us
    pallas_call x1, Pallas kernels: 10.3 us -> 9.83 us  [shards(): pl.pallas_call(functools.partial(kernel, groups, panels, stops), out_shap...]
where the time goes in v2:
time: 11.3 us; the launch traced here: 11.1 us
  Pallas kernels  9.83 us (87%)
  between operations  0.66 us (6%)
  local copies, waits for them, and re-layouts  0.63 us (6%)
    pallas_call x1, Pallas kernels, shards(): pl.pallas_call(functools.partial(kernel, groups, panels, stops), out_shap...  9.83 us
    unnamed x1, local copies, waits for them, and re-layouts  0.63 us

profile of v2, /device:TPU:0, one launch (start us, length us, event | category | flops | bytes accessed | tf_op | source)
XLA Modules:
  0.0 11.1 jit_solution(4034518485517236468)
XLA Ops:
  0.7 9.8 %shard_map.73 = bf16[2,128,128]{2,1,0:T(8,128)(2,1)S(1)} custom-call(bf16[16,1024]{1,0:T(8,128)(2,1)} %constant.2.clone.table_hbm, bf16[4,1024,128]{2,1,0:T(8,128)(2,1)} %raw_hbm.1, s32[4]{0:T(128)} %dest_hbm.1, s32[1]{0:T(128)S(6)} %copy.11.count_hbm, s32[2,64]{1,0:T(2,128)} %bitcast.6, bf16[2,64]{1,0:T(2,128)(2,1)} %bitcast.7, bf16[2,2,384]{2,1,0:T(2,128)(2,1)} %kern_hbm.1), custom_call_target="tpu_custom_call" | custom-call | tf_op jit(solution)/shard_map/pallas_call | solution.py:201
  10.5 0.6 %copy.10 = bf16[2,64,1,2,128]{4,3,2,1,0:T(2,128)(2,1)} copy(bf16[2,64,1,2,128]{4,3,2,1,0:T(2,128)(2,1)S(1)} %bitcast.5) | data formatting | bytes 131072

commit v3 on v2

v3 whole, which is shorter than its diff:
```python
import functools
import math

import jax
import jax.numpy as jnp
import numpy as np
from jax import lax
from jax.experimental import pallas as pl
from jax.experimental.pallas import tpu as pltpu
from jax.sharding import PartitionSpec as P

FLO = 32
MESH = pl.DeviceIdType.MESH
F32 = jnp.float32
BF16 = jnp.bfloat16


def dft_table(freq_count, sample_count, row_count):
    freqs = FLO + np.arange(freq_count, dtype=np.int32)
    samples = np.arange(sample_count, dtype=np.int32)
    angles = (freqs[:, None] * samples[None, :] % sample_count).astype(np.float32) * np.float32(
        2.0 * math.pi / sample_count
    )
    rows = np.stack([np.cos(angles), -np.sin(angles)], axis=1) / np.float32(math.sqrt(sample_count))
    table = np.zeros((row_count, sample_count), np.float32)
    table[: 2 * freq_count] = rows.reshape(2 * freq_count, sample_count)
    return jnp.asarray(table, BF16)


def kernel(
    groups, panels, stops,
    table_hbm, raw_hbm, dest_hbm, count_ref, stencil_hbm, weight_hbm, kern_hbm,
    out_ref,
    table, raw, dest, stencil, weight, kern, spectra, packed, received, operator,
    raw_sems, small_sems, shift_send_sems, shift_recv_sems, send_sem, recv_sem,
):
    raw_slots, _, width = raw.shape
    freq_count = kern.shape[0]
    rows = 2 * freq_count
    message_rows = packed.shape[1]
    shot_count = stencil.shape[1]
    back_reach = stops // 2 - 1
    my_group = lax.axis_index("acq")
    my_panel = lax.axis_index("rcv")

    small = [
        pltpu.make_async_copy(src, dst, small_sems.at[at])
        for at, (src, dst) in enumerate([
            (dest_hbm, dest), (stencil_hbm, stencil), (weight_hbm, weight), (table_hbm, table),
            (kern_hbm, kern),
        ])
    ]
    loads = [
        pltpu.make_async_copy(raw_hbm.at[j], raw.at[j], raw_sems.at[j]) for j in range(raw_slots)
    ]

    def moved(place, by, count):
        place = place + by
        if by < 0:
            return jnp.where(place < 0, place + count, place)
        return jnp.where(place >= count, place - count, place)

    def panel_at(offset):
        return {"acq": my_group, "rcv": moved(my_panel, offset, panels)}

    def group_at(step):
        return {"acq": moved(my_group, step, groups), "rcv": my_panel}

    far_stops = [stop for stop in range(stops) if stop != back_reach]
    barrier = pltpu.get_barrier_semaphore()
    for stop in far_stops:
        pl.semaphore_signal(
            barrier, inc=1, device_id=panel_at(stop - back_reach), device_id_type=MESH
        )
    for load in loads:
        load.start()
    for copy in small:
        copy.start()
    for step in range(1, groups):
        pl.semaphore_signal(barrier, inc=1, device_id=group_at(step), device_id_type=MESH)

    small[0].wait()
    select_shape = (groups * message_rows, stops * raw_slots * rows)
    select_row = lax.broadcasted_iota(jnp.int32, select_shape, 0)
    select_col = lax.broadcasted_iota(jnp.int32, select_shape, 1)
    owner_of = select_row // message_rows
    source = select_col // rows % raw_slots
    same_place = select_row % message_rows == (
        select_col // (raw_slots * rows) * rows + select_col % rows
    )
    target = jnp.full(select_shape, -1, jnp.int32)
    for j in range(raw_slots):
        target = jnp.where(source == j, jnp.where(j < count_ref[0], dest[j], -1), target)
    select = jnp.where(same_place & (owner_of == target), 1.0, 0.0).astype(BF16)

    small[1].wait()
    small[2].wait()
    tile = 8
    per_tile = tile // rows
    slot_at = lax.broadcasted_iota(jnp.int32, (groups * tile, shot_count), 0) // tile
    weights = weight[...].astype(F32)
    mixing = jnp.where(slot_at == stencil[0:1, :], weights[0:1, :], 0.0)
    mixing = mixing + jnp.where(slot_at == stencil[1:2, :], weights[1:2, :], 0.0)
    pairs = 2 * shot_count
    spread_rows = lax.broadcasted_iota(jnp.int32, (pairs, shot_count), 0)
    spread_cols = lax.broadcasted_iota(jnp.int32, (pairs, shot_count), 1)
    spread = jnp.where(spread_rows // 2 == spread_cols, 1.0, 0.0).astype(BF16)
    mixing = lax.dot_general(
        spread, mixing.astype(BF16), (((1,), (1,)), ((), ())), preferred_element_type=F32
    )
    part = lax.broadcasted_iota(jnp.int32, mixing.shape, 0) % 2
    signed = jnp.where(part == 0, mixing, -mixing)
    component = lax.broadcasted_iota(jnp.int32, mixing.shape, 1) % tile
    mixers = []
    for f in range(freq_count):
        for at in range(per_tile):
            first = at * rows + 2 * f
            mixers.append(jnp.where(component == first + part, mixing, 0.0).astype(BF16))
            mixers.append(jnp.where(component == first + 1 - part, signed, 0.0).astype(BF16))
    mixers = jnp.concatenate(mixers, axis=0)

    small[3].wait()
    pieces = []
    for first in range(0, raw_slots, 2):
        blocks = list(range(first, min(first + 2, raw_slots)))
        for j in blocks:
            loads[j].wait()
        pair = jnp.concatenate([raw[j] for j in blocks], axis=1)
        both = jnp.dot(table[...], pair, preferred_element_type=F32)
        for at in range(len(blocks)):
            pieces.append(both[:rows, at * width:(at + 1) * width])
    spectra[back_reach] = jnp.concatenate(pieces, axis=0).astype(BF16)

    pl.semaphore_wait(barrier, groups - 1 + stops - 1)
    shifts = [
        pltpu.make_async_remote_copy(
            src_ref=spectra.at[back_reach],
            dst_ref=spectra.at[stop],
            send_sem=shift_send_sems.at[stop],
            recv_sem=shift_recv_sems.at[stop],
            device_id=panel_at(back_reach - stop),
            device_id_type=MESH,
        )
        for stop in far_stops
    ]
    for shift in shifts:
        shift.start()

    lane = lax.broadcasted_iota(jnp.int32, (width, width), 1)
    row = lax.broadcasted_iota(jnp.int32, (width, width), 0)

    def fill_operator(f):
        for c in range(2):
            line = kern[f, c:c + 1, :].astype(F32)
            if c == 1:
                line = -line
            rolled = [
                pltpu.roll(
                    jnp.broadcast_to(line[:, at * width:(at + 1) * width], (width, width)),
                    0, 1, stride=1, stride_axis=0,
                )
                for at in range(stops + 1)
            ]
            for stop in range(stops):
                place = (2 * stop + c) * width
                operator[f, :, place:place + width] = jnp.where(
                    lane >= row, rolled[stop + 1], rolled[stop]
                ).astype(BF16)

    small[4].wait()
    for f in range(freq_count // 2):
        fill_operator(f)

    for shift in shifts:
        shift.wait_recv()
    gathered = jnp.dot(
        select, spectra[...].reshape(stops * raw_slots * rows, width), preferred_element_type=F32
    )
    packed[...] = gathered.reshape(groups, message_rows, width).astype(BF16)
    for step in range(1, groups):
        peer = group_at(step)
        pltpu.make_async_remote_copy(
            src_ref=packed.at[peer["acq"]],
            dst_ref=received.at[my_group],
            send_sem=send_sem,
            recv_sem=recv_sem,
            device_id=peer,
            device_id_type=MESH,
        ).start()
    received[my_group] = packed[my_group]
    for f in range(freq_count // 2, freq_count):
        fill_operator(f)

    arrived = received.at[pl.ds(0, groups - 1)]
    pltpu.make_async_copy(arrived, arrived, recv_sem).wait()
    slots = received[...].astype(F32)
    fields = [[] for _ in range(freq_count)]
    for first in range(0, stops, per_tile):
        start = first * rows
        part_slots = slots[:, start:start + tile].reshape(groups * tile, width).astype(BF16)
        regular = jnp.dot(mixers, part_slots, preferred_element_type=F32).astype(BF16)
        for f in range(freq_count):
            for at in range(2 * min(per_tile, stops - first)):
                place = (2 * f * per_tile + at) * pairs
                fields[f].append(regular[place:place + pairs])
    for f in range(freq_count):
        out_ref[f] = lax.dot_general(
            jnp.concatenate(fields[f], axis=1), operator[f], (((1,), (1,)), ((), ())),
            preferred_element_type=F32,
        ).astype(BF16)

    for shift in shifts:
        shift.wait_send()
    sent = packed.at[pl.ds(0, groups - 1)]
    pltpu.make_async_copy(sent, sent, send_sem).wait()


def shards(raw_blocks, raw_dest, raw_count, stencil, stencil_weight, kern):
    groups = lax.axis_size("acq")
    panels = lax.axis_size("rcv")
    stops = panels // 2
    raw_slots, sample_count, width = raw_blocks.shape
    freq_count = kern.shape[0]
    shot_count = stencil.shape[0]
    rows = 2 * freq_count
    message_rows = -(-stops * rows // 8) * 8
    table = dft_table(freq_count, sample_count, -(-rows // 16) * 16)
    args = (table, raw_blocks, raw_dest, raw_count, stencil.T, stencil_weight.T, kern)
    out = pl.pallas_call(
        functools.partial(kernel, groups, panels, stops),
        out_shape=pltpu.VMEM((freq_count, 2 * shot_count, width), BF16),
        in_specs=[
            pl.BlockSpec(memory_space=pltpu.SMEM if arg is raw_count else pltpu.HBM)
            for arg in args
        ],
        out_specs=pl.BlockSpec(memory_space=pltpu.VMEM),
        scratch_shapes=[
            pltpu.VMEM(table.shape, BF16),
            pltpu.VMEM(raw_blocks.shape, BF16),
            pltpu.SMEM(raw_dest.shape, jnp.int32),
            pltpu.VMEM((2, shot_count), jnp.int32),
            pltpu.VMEM((2, shot_count), BF16),
            pltpu.VMEM(kern.shape, BF16),
            pltpu.VMEM((stops, raw_slots * rows, width), BF16),
            pltpu.VMEM((groups, message_rows, width), BF16),
            pltpu.VMEM((groups, message_rows, width), BF16),
            pltpu.VMEM((freq_count, width, 2 * stops * width), BF16),
            pltpu.SemaphoreType.DMA((raw_slots,)),
            pltpu.SemaphoreType.DMA((5,)),
            pltpu.SemaphoreType.DMA((stops,)),
            pltpu.SemaphoreType.DMA((stops,)),
            pltpu.SemaphoreType.DMA,
            pltpu.SemaphoreType.DMA,
        ],
        compiler_params=pltpu.CompilerParams(
            collective_id=0, has_side_effects=True, vmem_limit_bytes=32 * 1024 * 1024
        ),
    )(*(
        arg if arg is raw_count else pltpu.with_memory_space_constraint(arg, pltpu.HBM)
        for arg in args
    ))
    return out.reshape(freq_count, shot_count, 1, 2, width)


def solution(mesh):
    return jax.shard_map(
        shards,
        mesh=mesh,
        in_specs=(P("acq", None, "rcv"), P("acq"), P("acq"), P("acq", None), P("acq", None), P()),
        out_specs=P(None, "acq", "rcv", None, None),
        check_vma=False,
    )
```

time: 11.3 us -> 12.3 us (1.088)
  Pallas kernels: 9.83 us -> 10.9 us
    pallas_call x1, Pallas kernels: 9.83 us -> 10.9 us  [shards(): pl.pallas_call(functools.partial(kernel, groups, panels, stops), out_shap...]
where the time goes in v3:
time: 12.3 us; the launch traced here: 12.1 us
  Pallas kernels  10.9 us (89%)
  between operations  0.66 us (5%)
  local copies, waits for them, and re-layouts  0.63 us (5%)
    pallas_call x1, Pallas kernels, shards(): pl.pallas_call(functools.partial(kernel, groups, panels, stops), out_shap...  10.9 us
    unnamed x1, local copies, waits for them, and re-layouts  0.63 us

profile of v3, /device:TPU:0, one launch (start us, length us, event | category | flops | bytes accessed | tf_op | source)
XLA Modules:
  0.0 12.1 jit_solution(11654377069774946672)
XLA Ops:
  0.7 10.9 %shard_map.73 = bf16[2,128,128]{2,1,0:T(8,128)(2,1)S(1)} custom-call(bf16[16,1024]{1,0:T(8,128)(2,1)} %constant.2.clone.table_hbm, bf16[4,1024,128]{2,1,0:T(8,128)(2,1)} %raw_hbm.1, s32[4]{0:T(128)} %dest_hbm.1, s32[1]{0:T(128)S(6)} %copy.11.count_ref, s32[2,64]{1,0:T(2,128)} %bitcast.6, bf16[2,64]{1,0:T(2,128)(2,1)} %bitcast.7, bf16[2,2,384]{2,1,0:T(2,128)(2,1)} %kern_hbm.1), custom_call_target="tpu_custom_call" | custom-call | tf_op jit(solution)/shard_map/pallas_call | solution.py:229
  11.5 0.6 %copy.10 = bf16[2,64,1,2,128]{4,3,2,1,0:T(2,128)(2,1)} copy(bf16[2,64,1,2,128]{4,3,2,1,0:T(2,128)(2,1)S(1)} %bitcast.5) | data formatting | bytes 131072

commit v4 on v3

--- a/solution.py
+++ b/solution.py
@@ -27,6 +27,12 @@
     return jnp.asarray(table, BF16)
 
 
+def split(index, size):
+    if size & (size - 1):
+        return index // size, index % size
+    return index >> (size.bit_length() - 1), index & (size - 1)
+
+
 def kernel(
     groups, panels, stops,
     table_hbm, raw_hbm, dest_hbm, count_ref, stencil_hbm, weight_hbm, kern_hbm,
@@ -34,7 +40,8 @@
     table, raw, dest, stencil, weight, kern, spectra, packed, received, operator,
     raw_sems, small_sems, shift_send_sems, shift_recv_sems, send_sem, recv_sem,
 ):
-    raw_slots, _, width = raw.shape
+    raw_slots, sample_count, width = raw.shape
+    depth = sample_count // raw_sems.shape[1]
     freq_count = kern.shape[0]
     rows = 2 * freq_count
     message_rows = packed.shape[1]
@@ -51,7 +58,14 @@
         ])
     ]
     loads = [
-        pltpu.make_async_copy(raw_hbm.at[j], raw.at[j], raw_sems.at[j]) for j in range(raw_slots)
+        [
+            pltpu.make_async_copy(
+                raw_hbm.at[j, pl.ds(first, depth)], raw.at[j, pl.ds(first, depth)],
+                raw_sems.at[j, at],
+            )
+            for at, first in enumerate(range(0, sample_count, depth))
+        ]
+        for j in range(raw_slots)
     ]
 
     def moved(place, by, count):
@@ -72,8 +86,9 @@
         pl.semaphore_signal(
             barrier, inc=1, device_id=panel_at(stop - back_reach), device_id_type=MESH
         )
-    for load in loads:
-        load.start()
+    for block in loads:
+        for load in block:
+            load.start()
     for copy in small:
         copy.start()
     for step in range(1, groups):
@@ -83,50 +98,29 @@
     select_shape = (groups * message_rows, stops * raw_slots * rows)
     select_row = lax.broadcasted_iota(jnp.int32, select_shape, 0)
     select_col = lax.broadcasted_iota(jnp.int32, select_shape, 1)
-    owner_of = select_row // message_rows
-    source = select_col // rows % raw_slots
-    same_place = select_row % message_rows == (
-        select_col // (raw_slots * rows) * rows + select_col % rows
-    )
+    owner_of, message_row = split(select_row, message_rows)
+    block_of, source_row = split(select_col, rows)
+    source_stop, source = split(block_of, raw_slots)
+    same_place = message_row == source_stop * rows + source_row
     target = jnp.full(select_shape, -1, jnp.int32)
     for j in range(raw_slots):
         target = jnp.where(source == j, jnp.where(j < count_ref[0], dest[j], -1), target)
     select = jnp.where(same_place & (owner_of == target), 1.0, 0.0).astype(BF16)
 
-    small[1].wait()
-    small[2].wait()
-    tile = 8
-    per_tile = tile // rows
-    slot_at = lax.broadcasted_iota(jnp.int32, (groups * tile, shot_count), 0) // tile
-    weights = weight[...].astype(F32)
-    mixing = jnp.where(slot_at == stencil[0:1, :], weights[0:1, :], 0.0)
-    mixing = mixing + jnp.where(slot_at == stencil[1:2, :], weights[1:2, :], 0.0)
-    pairs = 2 * shot_count
-    spread_rows = lax.broadcasted_iota(jnp.int32, (pairs, shot_count), 0)
-    spread_cols = lax.broadcasted_iota(jnp.int32, (pairs, shot_count), 1)
-    spread = jnp.where(spread_rows // 2 == spread_cols, 1.0, 0.0).astype(BF16)
-    mixing = lax.dot_general(
-        spread, mixing.astype(BF16), (((1,), (1,)), ((), ())), preferred_element_type=F32
-    )
-    part = lax.broadcasted_iota(jnp.int32, mixing.shape, 0) % 2
-    signed = jnp.where(part == 0, mixing, -mixing)
-    component = lax.broadcasted_iota(jnp.int32, mixing.shape, 1) % tile
-    mixers = []
-    for f in range(freq_count):
-        for at in range(per_tile):
-            first = at * rows + 2 * f
-            mixers.append(jnp.where(component == first + part, mixing, 0.0).astype(BF16))
-            mixers.append(jnp.where(component == first + 1 - part, signed, 0.0).astype(BF16))
-    mixers = jnp.concatenate(mixers, axis=0)
-
     small[3].wait()
     pieces = []
     for first in range(0, raw_slots, 2):
         blocks = list(range(first, min(first + 2, raw_slots)))
-        for j in blocks:
-            loads[j].wait()
-        pair = jnp.concatenate([raw[j] for j in blocks], axis=1)
-        both = jnp.dot(table[...], pair, preferred_element_type=F32)
+        both = None
+        for at in range(sample_count // depth):
+            for j in blocks:
+                loads[j][at].wait()
+            span = slice(at * depth, (at + 1) * depth)
+            term = jnp.dot(
+                table[:, span], jnp.concatenate([raw[j, span] for j in blocks], axis=1),
+                preferred_element_type=F32,
+            )
+            both = term if both is None else both + term
         for at in range(len(blocks)):
             pieces.append(both[:rows, at * width:(at + 1) * width])
     spectra[back_reach] = jnp.concatenate(pieces, axis=0).astype(BF16)
@@ -146,30 +140,56 @@
     for shift in shifts:
         shift.start()
 
+    small[1].wait()
+    small[2].wait()
+    tile = 8
+    per_tile = tile // rows
+    slot_at, _ = split(lax.broadcasted_iota(jnp.int32, (groups * tile, shot_count), 0), tile)
+    weights = weight[...].astype(F32)
+    mixing = jnp.where(slot_at == stencil[0:1, :], weights[0:1, :], 0.0)
+    mixing = mixing + jnp.where(slot_at == stencil[1:2, :], weights[1:2, :], 0.0)
+    pairs = 2 * shot_count
+    spread_rows = lax.broadcasted_iota(jnp.int32, (pairs, shot_count), 0)
+    spread_cols = lax.broadcasted_iota(jnp.int32, (pairs, shot_count), 1)
+    spread = jnp.where(split(spread_rows, 2)[0] == spread_cols, 1.0, 0.0).astype(BF16)
+    mixing = lax.dot_general(
+        spread, mixing.astype(BF16), (((1,), (1,)), ((), ())), preferred_element_type=F32
+    )
+    _, part = split(lax.broadcasted_iota(jnp.int32, mixing.shape, 0), 2)
+    signed = jnp.where(part == 0, mixing, -mixing)
+    _, component = split(lax.broadcasted_iota(jnp.int32, mixing.shape, 1), tile)
+    mixers = []
+    for f in range(freq_count):
+        for at in range(per_tile):
+            first = at * rows + 2 * f
+            mixers.append(jnp.where(component == first + part, mixing, 0.0).astype(BF16))
+            mixers.append(jnp.where(component == first + 1 - part, signed, 0.0).astype(BF16))
+    mixers = jnp.concatenate(mixers, axis=0)
+
+    small[4].wait()
     lane = lax.broadcasted_iota(jnp.int32, (width, width), 1)
     row = lax.broadcasted_iota(jnp.int32, (width, width), 0)
-
-    def fill_operator(f):
+    flip = jnp.where(lane + row == width - 1, 1.0, 0.0).astype(BF16)
+    lines = jnp.concatenate([kern[f].astype(F32) for f in range(freq_count)], axis=0).astype(BF16)
+    flipped = [
+        jnp.dot(lines[:, at * width:(at + 1) * width], flip, preferred_element_type=F32)
+        for at in range(stops + 1)
+    ]
+    for f in range(freq_count):
         for c in range(2):
-            line = kern[f, c:c + 1, :].astype(F32)
-            if c == 1:
-                line = -line
-            rolled = [
-                pltpu.roll(
-                    jnp.broadcast_to(line[:, at * width:(at + 1) * width], (width, width)),
-                    0, 1, stride=1, stride_axis=0,
-                )
-                for at in range(stops + 1)
-            ]
+            line = 2 * f + c
+            rolled = []
+            for at in range(stops + 1):
+                piece = flipped[at][line:line + 1]
+                piece = -piece if c == 1 else piece
+                rolled.append(pltpu.roll(
+                    jnp.broadcast_to(piece, (width, width)), 1, 1, stride=1, stride_axis=0
+                ))
             for stop in range(stops):
                 place = (2 * stop + c) * width
-                operator[f, :, place:place + width] = jnp.where(
-                    lane >= row, rolled[stop + 1], rolled[stop]
+                operator[f, place:place + width] = jnp.where(
+                    row >= lane, rolled[stop + 1], rolled[stop]
                 ).astype(BF16)
-
-    small[4].wait()
-    for f in range(freq_count // 2):
-        fill_operator(f)
 
     for shift in shifts:
         shift.wait_recv()
@@ -188,8 +208,6 @@
             device_id_type=MESH,
         ).start()
     received[my_group] = packed[my_group]
-    for f in range(freq_count // 2, freq_count):
-        fill_operator(f)
 
     arrived = received.at[pl.ds(0, groups - 1)]
     pltpu.make_async_copy(arrived, arrived, recv_sem).wait()
@@ -204,9 +222,8 @@
                 place = (2 * f * per_tile + at) * pairs
                 fields[f].append(regular[place:place + pairs])
     for f in range(freq_count):
-        out_ref[f] = lax.dot_general(
-            jnp.concatenate(fields[f], axis=1), operator[f], (((1,), (1,)), ((), ())),
-            preferred_element_type=F32,
+        out_ref[f] = jnp.dot(
+            jnp.concatenate(fields[f], axis=1), operator[f], preferred_element_type=F32
         ).astype(BF16)
 
     for shift in shifts:
@@ -244,8 +261,8 @@
             pltpu.VMEM((stops, raw_slots * rows, width), BF16),
             pltpu.VMEM((groups, message_rows, width), BF16),
             pltpu.VMEM((groups, message_rows, width), BF16),
-            pltpu.VMEM((freq_count, width, 2 * stops * width), BF16),
-            pltpu.SemaphoreType.DMA((raw_slots,)),
+            pltpu.VMEM((freq_count, 2 * stops * width, width), BF16),
+            pltpu.SemaphoreType.DMA((raw_slots, 2)),
             pltpu.SemaphoreType.DMA((5,)),
             pltpu.SemaphoreType.DMA((stops,)),
             pltpu.SemaphoreType.DMA((stops,)),

time: 12.3 us -> 12.5 us (1.016)
    pallas_call x1, Pallas kernels: 10.9 us -> 11 us  [shards(): pl.pallas_call(functools.partial(kernel, groups, panels, stops), out_shap...]
where the time goes in v4:
time: 12.5 us; the launch traced here: 12.3 us
  Pallas kernels  11 us (88%)
  between operations  0.66 us (5%)
  local copies, waits for them, and re-layouts  0.63 us (5%)
    pallas_call x1, Pallas kernels, shards(): pl.pallas_call(functools.partial(kernel, groups, panels, stops), out_shap...  11 us
    unnamed x1, local copies, waits for them, and re-layouts  0.63 us

profile of v4, /device:TPU:0, one launch (start us, length us, event | category | flops | bytes accessed | tf_op | source)
XLA Modules:
  0.0 12.3 jit_solution(11980081412480321990)
XLA Ops:
  0.7 11.0 %shard_map.73 = bf16[2,128,128]{2,1,0:T(8,128)(2,1)S(1)} custom-call(bf16[16,1024]{1,0:T(8,128)(2,1)} %constant.2.clone.table_hbm, bf16[4,1024,128]{2,1,0:T(8,128)(2,1)} %raw_hbm.1, s32[4]{0:T(128)} %dest_hbm.1, s32[1]{0:T(128)S(6)} %copy.11.count_ref, s32[2,64]{1,0:T(2,128)} %bitcast.6, bf16[2,64]{1,0:T(2,128)(2,1)} %bitcast.7, bf16[2,2,384]{2,1,0:T(2,128)(2,1)} %kern_hbm.1), custom_call_target="tpu_custom_call" | custom-call | tf_op jit(solution)/shard_map/pallas_call | solution.py:246
  11.7 0.6 %copy.10 = bf16[2,64,1,2,128]{4,3,2,1,0:T(2,128)(2,1)} copy(bf16[2,64,1,2,128]{4,3,2,1,0:T(2,128)(2,1)S(1)} %bitcast.5) | data formatting | bytes 131072

commit v5 on v4

v5 whole, which is shorter than its diff:
```python
import functools
import math

import jax
import jax.numpy as jnp
import numpy as np
from jax import lax
from jax.experimental import pallas as pl
from jax.experimental.pallas import tpu as pltpu
from jax.sharding import PartitionSpec as P

FLO = 32
MESH = pl.DeviceIdType.MESH
F32 = jnp.float32
BF16 = jnp.bfloat16


def dft_table(freq_count, sample_count, row_count):
    freqs = FLO + np.arange(freq_count, dtype=np.int32)
    samples = np.arange(sample_count, dtype=np.int32)
    angles = (freqs[:, None] * samples[None, :] % sample_count).astype(np.float32) * np.float32(
        2.0 * math.pi / sample_count
    )
    rows = np.stack([np.cos(angles), -np.sin(angles)], axis=1) / np.float32(math.sqrt(sample_count))
    table = np.zeros((row_count, sample_count), np.float32)
    table[: 2 * freq_count] = rows.reshape(2 * freq_count, sample_count)
    return jnp.asarray(table, BF16)


def split(index, size):
    if size & (size - 1):
        return index // size, index % size
    return index >> (size.bit_length() - 1), index & (size - 1)


def kernel(
    groups, panels, stops,
    table_hbm, raw_hbm, dest_hbm, count_ref, stencil_hbm, weight_hbm, kern_hbm,
    out_ref,
    table, raw, dest, stencil, weight, kern, packed, received, slots, operator,
    raw_sems, small_sems, send_sem, recv_sems,
):
    raw_slots, sample_count, width = raw.shape
    depth = sample_count // raw_sems.shape[1]
    freq_count = kern.shape[0]
    rows = 2 * freq_count
    tile = -(-rows // 8) * 8
    shot_count = stencil.shape[1]
    back_reach = stops // 2 - 1
    my_group = lax.axis_index("acq")
    my_panel = lax.axis_index("rcv")

    small = [
        pltpu.make_async_copy(src, dst, small_sems.at[at])
        for at, (src, dst) in enumerate([
            (dest_hbm, dest), (stencil_hbm, stencil), (weight_hbm, weight), (table_hbm, table),
            (kern_hbm, kern),
        ])
    ]
    loads = [
        [
            pltpu.make_async_copy(
                raw_hbm.at[j, pl.ds(first, depth)], raw.at[j, pl.ds(first, depth)],
                raw_sems.at[j, at],
            )
            for at, first in enumerate(range(0, sample_count, depth))
        ]
        for j in range(raw_slots)
    ]

    def moved(place, by, count):
        place = place + by
        if by < 0:
            return jnp.where(place < 0, place + count, place)
        return jnp.where(place >= count, place - count, place)

    far_first = sorted(range(stops), key=lambda stop: -abs(stop - back_reach))

    def peers(sign):
        for stop in far_first:
            panel = moved(my_panel, sign * (stop - back_reach), panels)
            for step in range(groups):
                if stop != back_reach or step != 0:
                    group = moved(my_group, step, groups)
                    yield stop, group, {"acq": group, "rcv": panel}

    barrier = pltpu.get_barrier_semaphore()
    for _, _, peer in peers(1):
        pl.semaphore_signal(barrier, inc=1, device_id=peer, device_id_type=MESH)
    for block in loads:
        for load in block:
            load.start()
    for copy in small:
        copy.start()
    slots[...] = jnp.zeros_like(slots)
    small[0].wait()
    select_shape = (groups * tile, raw_slots * rows)
    owner_of, place_row = split(lax.broadcasted_iota(jnp.int32, select_shape, 0), tile)
    source, source_row = split(lax.broadcasted_iota(jnp.int32, select_shape, 1), rows)
    same_place = place_row == source_row
    target = jnp.full(select_shape, -1, jnp.int32)
    for j in range(raw_slots):
        target = jnp.where(source == j, jnp.where(j < count_ref[0], dest[j], -1), target)
    select = jnp.where(same_place & (owner_of == target), 1.0, 0.0).astype(BF16)

    small[1].wait()
    small[2].wait()
    slot_at, _ = split(lax.broadcasted_iota(jnp.int32, (groups * tile, shot_count), 0), tile)
    weights = weight[...].astype(F32)
    mixing = jnp.where(slot_at == stencil[0:1, :], weights[0:1, :], 0.0)
    mixing = mixing + jnp.where(slot_at == stencil[1:2, :], weights[1:2, :], 0.0)
    pairs = 2 * shot_count
    spread_rows = lax.broadcasted_iota(jnp.int32, (pairs, shot_count), 0)
    spread_cols = lax.broadcasted_iota(jnp.int32, (pairs, shot_count), 1)
    spread = jnp.where(split(spread_rows, 2)[0] == spread_cols, 1.0, 0.0).astype(BF16)
    mixing = lax.dot_general(
        spread, mixing.astype(BF16), (((1,), (1,)), ((), ())), preferred_element_type=F32
    )
    _, part = split(lax.broadcasted_iota(jnp.int32, mixing.shape, 0), 2)
    signed = jnp.where(part == 0, mixing, -mixing)
    _, component = split(lax.broadcasted_iota(jnp.int32, mixing.shape, 1), tile)
    mixers = []
    for f in range(freq_count):
        mixers.append(jnp.where(component == 2 * f + part, mixing, 0.0).astype(BF16))
        mixers.append(jnp.where(component == 2 * f + 1 - part, signed, 0.0).astype(BF16))
    mixers = jnp.concatenate(mixers, axis=0)

    small[4].wait()
    lane = lax.broadcasted_iota(jnp.int32, (width, width), 1)
    row = lax.broadcasted_iota(jnp.int32, (width, width), 0)
    flip = jnp.where(lane + row == width - 1, 1.0, 0.0).astype(BF16)
    lines = jnp.concatenate([kern[f].astype(F32) for f in range(freq_count)], axis=0).astype(BF16)
    flipped = [
        jnp.dot(lines[:, at * width:(at + 1) * width], flip, preferred_element_type=F32)
        for at in range(stops + 1)
    ]
    for f in range(freq_count):
        for c in range(2):
            line = 2 * f + c
            rolled = []
            for at in range(stops + 1):
                piece = flipped[at][line:line + 1]
                piece = -piece if c == 1 else piece
                rolled.append(pltpu.roll(
                    jnp.broadcast_to(piece, (width, width)), 1, 1, stride=1, stride_axis=0
                ))
            for stop in range(stops):
                place = (2 * stop + c) * width
                operator[f, place:place + width] = jnp.where(
                    row >= lane, rolled[stop + 1], rolled[stop]
                ).astype(BF16)

    small[3].wait()
    pieces = []
    for first in range(0, raw_slots, 2):
        blocks = list(range(first, min(first + 2, raw_slots)))
        both = None
        for at in range(sample_count // depth):
            for j in blocks:
                loads[j][at].wait()
            span = slice(at * depth, (at + 1) * depth)
            term = jnp.dot(
                table[:, span], jnp.concatenate([raw[j, span] for j in blocks], axis=1),
                preferred_element_type=F32,
            )
            both = term if both is None else both + term
        for at in range(len(blocks)):
            pieces.append(both[:rows, at * width:(at + 1) * width])
    spectra = jnp.concatenate(pieces, axis=0).astype(BF16)
    gathered = jnp.dot(select, spectra, preferred_element_type=F32)
    for owner in range(groups):
        packed[owner] = gathered[owner * tile:owner * tile + rows].astype(BF16)

    pl.semaphore_wait(barrier, groups * stops - 1)
    for stop, group, peer in peers(-1):
        pltpu.make_async_remote_copy(
            src_ref=packed.at[group],
            dst_ref=received.at[stop, my_group],
            send_sem=send_sem,
            recv_sem=recv_sems.at[stop],
            device_id=peer,
            device_id_type=MESH,
        ).start()
    received[back_reach, my_group] = packed[my_group]

    totals = [jnp.zeros((pairs, width), F32)] * freq_count
    for stop in reversed(far_first):
        arrived = received.at[stop]
        if stop == back_reach:
            arrived = received.at[stop, pl.ds(0, groups - 1)]
        pltpu.make_async_copy(arrived, arrived, recv_sems.at[stop]).wait()
        for group in range(groups):
            slots[stop, group * tile:group * tile + rows] = received[stop, group].astype(F32)
        regular = jnp.dot(
            mixers, slots[stop].astype(BF16), preferred_element_type=F32
        ).astype(BF16)
        for f in range(freq_count):
            at = 2 * f * pairs
            fields = jnp.concatenate(
                [regular[at:at + pairs], regular[at + pairs:at + 2 * pairs]], axis=1
            )
            totals[f] = totals[f] + jnp.dot(
                fields, operator[f, 2 * stop * width:2 * (stop + 1) * width],
                preferred_element_type=F32,
            )
    for f in range(freq_count):
        out_ref[f] = totals[f].astype(BF16)

    for stop in range(stops):
        sent = packed
        if stop == back_reach:
            sent = packed.at[pl.ds(0, groups - 1)]
        pltpu.make_async_copy(sent, sent, send_sem).wait()


def shards(raw_blocks, raw_dest, raw_count, stencil, stencil_weight, kern):
    groups = lax.axis_size("acq")
    panels = lax.axis_size("rcv")
    stops = panels // 2
    raw_slots, sample_count, width = raw_blocks.shape
    freq_count = kern.shape[0]
    shot_count = stencil.shape[0]
    rows = 2 * freq_count
    tile = -(-rows // 8) * 8
    table = dft_table(freq_count, sample_count, -(-rows // 16) * 16)
    args = (table, raw_blocks, raw_dest, raw_count, stencil.T, stencil_weight.T, kern)
    out = pl.pallas_call(
        functools.partial(kernel, groups, panels, stops),
        out_shape=pltpu.VMEM((freq_count, 2 * shot_count, width), BF16),
        in_specs=[
            pl.BlockSpec(memory_space=pltpu.SMEM if arg is raw_count else pltpu.HBM)
            for arg in args
        ],
        out_specs=pl.BlockSpec(memory_space=pltpu.VMEM),
        scratch_shapes=[
            pltpu.VMEM(table.shape, BF16),
            pltpu.VMEM(raw_blocks.shape, BF16),
            pltpu.SMEM(raw_dest.shape, jnp.int32),
            pltpu.VMEM((2, shot_count), jnp.int32),
            pltpu.VMEM((2, shot_count), BF16),
            pltpu.VMEM(kern.shape, BF16),
            pltpu.VMEM((groups, rows, width), BF16),
            pltpu.VMEM((stops, groups, rows, width), BF16),
            pltpu.VMEM((stops, groups * tile, width), F32),
            pltpu.VMEM((freq_count, 2 * stops * width, width), BF16),
            pltpu.SemaphoreType.DMA((raw_slots, 2)),
            pltpu.SemaphoreType.DMA((5,)),
            pltpu.SemaphoreType.DMA,
            pltpu.SemaphoreType.DMA((stops,)),
        ],
        compiler_params=pltpu.CompilerParams(
            collective_id=0, has_side_effects=True, vmem_limit_bytes=32 * 1024 * 1024
        ),
    )(*(
        arg if arg is raw_count else pltpu.with_memory_space_constraint(arg, pltpu.HBM)
        for arg in args
    ))
    return out.reshape(freq_count, shot_count, 1, 2, width)


def solution(mesh):
    return jax.shard_map(
        shards,
        mesh=mesh,
        in_specs=(P("acq", None, "rcv"), P("acq"), P("acq"), P("acq", None), P("acq", None), P()),
        out_specs=P(None, "acq", "rcv", None, None),
        check_vma=False,
    )
```

time: 12.5 us -> 11.3 us (0.904)
  Pallas kernels: 11 us -> 9.83 us
    pallas_call x1, Pallas kernels: 11 us -> 9.83 us  [shards(): pl.pallas_call(functools.partial(kernel, groups, panels, stops), out_shap...]
where the time goes in v5:
time: 11.3 us; the launch traced here: 11.1 us
  Pallas kernels  9.83 us (87%)
  between operations  0.66 us (6%)
  local copies, waits for them, and re-layouts  0.63 us (6%)
    pallas_call x1, Pallas kernels, shards(): pl.pallas_call(functools.partial(kernel, groups, panels, stops), out_shap...  9.83 us
    unnamed x1, local copies, waits for them, and re-layouts  0.63 us

profile of v5, /device:TPU:0, one launch (start us, length us, event | category | flops | bytes accessed | tf_op | source)
XLA Modules:
  0.0 11.1 jit_solution(3266566090823062824)
XLA Ops:
  0.7 9.8 %shard_map.73 = bf16[2,128,128]{2,1,0:T(8,128)(2,1)S(1)} custom-call(bf16[16,1024]{1,0:T(8,128)(2,1)} %constant.2.clone.table_hbm, bf16[4,1024,128]{2,1,0:T(8,128)(2,1)} %raw_hbm.1, s32[4]{0:T(128)} %dest_hbm.1, s32[1]{0:T(128)S(6)} %copy.11.count_ref, s32[2,64]{1,0:T(2,128)} %bitcast.6, bf16[2,64]{1,0:T(2,128)(2,1)} %bitcast.7, bf16[2,2,384]{2,1,0:T(2,128)(2,1)} %kern_hbm.1), custom_call_target="tpu_custom_call" | custom-call | tf_op jit(solution)/shard_map/pallas_call | solution.py:227
  10.5 0.6 %copy.10 = bf16[2,64,1,2,128]{4,3,2,1,0:T(2,128)(2,1)} copy(bf16[2,64,1,2,128]{4,3,2,1,0:T(2,128)(2,1)S(1)} %bitcast.5) | data formatting | bytes 131072

commit v6 on v5

--- a/solution.py
+++ b/solution.py
@@ -37,8 +37,8 @@
     groups, panels, stops,
     table_hbm, raw_hbm, dest_hbm, count_ref, stencil_hbm, weight_hbm, kern_hbm,
     out_ref,
-    table, raw, dest, stencil, weight, kern, packed, received, slots, operator,
-    raw_sems, small_sems, send_sem, recv_sems,
+    table, raw, dest, stencil, weight, kern, packed, received, relay, slots, mixers, operator,
+    raw_sems, small_sems, send_sem, recv_sems, relay_sems,
 ):
     raw_slots, sample_count, width = raw.shape
     depth = sample_count // raw_sems.shape[1]
@@ -46,6 +46,7 @@
     rows = 2 * freq_count
     tile = -(-rows // 8) * 8
     shot_count = stencil.shape[1]
+    pairs = 2 * shot_count
     back_reach = stops // 2 - 1
     my_group = lax.axis_index("acq")
     my_panel = lax.axis_index("rcv")
@@ -84,9 +85,29 @@
                     group = moved(my_group, step, groups)
                     yield stop, group, {"acq": group, "rcv": panel}
 
+    relayed = stops == 2 and panels >= 4
+    last = panels - 1
+    relay_panel = panels - 2
     barrier = pltpu.get_barrier_semaphore()
-    for _, _, peer in peers(1):
-        pl.semaphore_signal(barrier, inc=1, device_id=peer, device_id_type=MESH)
+
+    def greet(group, panel):
+        pl.semaphore_signal(
+            barrier, inc=1, device_id={"acq": group, "rcv": panel}, device_id_type=MESH
+        )
+
+    if relayed:
+        @pl.when(my_panel == relay_panel)
+        def _():
+            greet(my_group, 0)
+
+        sender_panel = jnp.where(my_panel == last, relay_panel, my_panel + 1)
+        for step in range(groups):
+            greet(moved(my_group, step, groups), sender_panel)
+        for step in range(1, groups):
+            greet(moved(my_group, step, groups), my_panel)
+    else:
+        for _, group, peer in peers(1):
+            greet(group, peer["rcv"])
     for block in loads:
         for load in block:
             load.start()
@@ -103,53 +124,58 @@
         target = jnp.where(source == j, jnp.where(j < count_ref[0], dest[j], -1), target)
     select = jnp.where(same_place & (owner_of == target), 1.0, 0.0).astype(BF16)
 
-    small[1].wait()
-    small[2].wait()
-    slot_at, _ = split(lax.broadcasted_iota(jnp.int32, (groups * tile, shot_count), 0), tile)
-    weights = weight[...].astype(F32)
-    mixing = jnp.where(slot_at == stencil[0:1, :], weights[0:1, :], 0.0)
-    mixing = mixing + jnp.where(slot_at == stencil[1:2, :], weights[1:2, :], 0.0)
-    pairs = 2 * shot_count
-    spread_rows = lax.broadcasted_iota(jnp.int32, (pairs, shot_count), 0)
-    spread_cols = lax.broadcasted_iota(jnp.int32, (pairs, shot_count), 1)
-    spread = jnp.where(split(spread_rows, 2)[0] == spread_cols, 1.0, 0.0).astype(BF16)
-    mixing = lax.dot_general(
-        spread, mixing.astype(BF16), (((1,), (1,)), ((), ())), preferred_element_type=F32
-    )
-    _, part = split(lax.broadcasted_iota(jnp.int32, mixing.shape, 0), 2)
-    signed = jnp.where(part == 0, mixing, -mixing)
-    _, component = split(lax.broadcasted_iota(jnp.int32, mixing.shape, 1), tile)
-    mixers = []
-    for f in range(freq_count):
-        mixers.append(jnp.where(component == 2 * f + part, mixing, 0.0).astype(BF16))
-        mixers.append(jnp.where(component == 2 * f + 1 - part, signed, 0.0).astype(BF16))
-    mixers = jnp.concatenate(mixers, axis=0)
-
-    small[4].wait()
-    lane = lax.broadcasted_iota(jnp.int32, (width, width), 1)
-    row = lax.broadcasted_iota(jnp.int32, (width, width), 0)
-    flip = jnp.where(lane + row == width - 1, 1.0, 0.0).astype(BF16)
-    lines = jnp.concatenate([kern[f].astype(F32) for f in range(freq_count)], axis=0).astype(BF16)
-    flipped = [
-        jnp.dot(lines[:, at * width:(at + 1) * width], flip, preferred_element_type=F32)
-        for at in range(stops + 1)
-    ]
-    for f in range(freq_count):
-        for c in range(2):
-            line = 2 * f + c
-            rolled = []
-            for at in range(stops + 1):
-                piece = flipped[at][line:line + 1]
-                piece = -piece if c == 1 else piece
-                rolled.append(pltpu.roll(
-                    jnp.broadcast_to(piece, (width, width)), 1, 1, stride=1, stride_axis=0
-                ))
-            for stop in range(stops):
-                place = (2 * stop + c) * width
-                operator[f, place:place + width] = jnp.where(
-                    row >= lane, rolled[stop + 1], rolled[stop]
-                ).astype(BF16)
-
+    def prepare():
+        small[1].wait()
+        small[2].wait()
+        slot_at, _ = split(lax.broadcasted_iota(jnp.int32, (groups * tile, shot_count), 0), tile)
+        weights = weight[...].astype(F32)
+        mixing = jnp.where(slot_at == stencil[0:1, :], weights[0:1, :], 0.0)
+        mixing = mixing + jnp.where(slot_at == stencil[1:2, :], weights[1:2, :], 0.0)
+        spread_rows = lax.broadcasted_iota(jnp.int32, (pairs, shot_count), 0)
+        spread_cols = lax.broadcasted_iota(jnp.int32, (pairs, shot_count), 1)
+        spread = jnp.where(split(spread_rows, 2)[0] == spread_cols, 1.0, 0.0).astype(BF16)
+        mixing = lax.dot_general(
+            spread, mixing.astype(BF16), (((1,), (1,)), ((), ())), preferred_element_type=F32
+        )
+        _, part = split(lax.broadcasted_iota(jnp.int32, mixing.shape, 0), 2)
+        signed = jnp.where(part == 0, mixing, -mixing)
+        _, component = split(lax.broadcasted_iota(jnp.int32, mixing.shape, 1), tile)
+        for f in range(freq_count):
+            mixers[2 * f * pairs:(2 * f + 1) * pairs] = (
+                jnp.where(component == 2 * f + part, mixing, 0.0).astype(BF16)
+            )
+            mixers[(2 * f + 1) * pairs:(2 * f + 2) * pairs] = (
+                jnp.where(component == 2 * f + 1 - part, signed, 0.0).astype(BF16)
+            )
+
+        small[4].wait()
+        lane = lax.broadcasted_iota(jnp.int32, (width, width), 1)
+        row = lax.broadcasted_iota(jnp.int32, (width, width), 0)
+        flip = jnp.where(lane + row == width - 1, 1.0, 0.0).astype(BF16)
+        lines = jnp.concatenate([kern[f].astype(F32) for f in range(freq_count)], axis=0).astype(BF16)
+        flipped = [
+            jnp.dot(lines[:, at * width:(at + 1) * width], flip, preferred_element_type=F32)
+            for at in range(stops + 1)
+        ]
+        for f in range(freq_count):
+            for c in range(2):
+                line = 2 * f + c
+                rolled = []
+                for at in range(stops + 1):
+                    piece = flipped[at][line:line + 1]
+                    piece = -piece if c == 1 else piece
+                    rolled.append(pltpu.roll(
+                        jnp.broadcast_to(piece, (width, width)), 1, 1, stride=1, stride_axis=0
+                    ))
+                for stop in range(stops):
+                    place = (2 * stop + c) * width
+                    operator[f, place:place + width] = jnp.where(
+                        row >= lane, rolled[stop + 1], rolled[stop]
+                    ).astype(BF16)
+
+    if relayed:
+        waits_long = (my_panel == 0) | (my_panel == relay_panel)
+        pl.when(waits_long)(prepare)
     small[3].wait()
     pieces = []
     for first in range(0, raw_slots, 2):
@@ -171,17 +197,63 @@
     for owner in range(groups):
         packed[owner] = gathered[owner * tile:owner * tile + rows].astype(BF16)
 
-    pl.semaphore_wait(barrier, groups * stops - 1)
-    for stop, group, peer in peers(-1):
+    def send(src, dst, send_to, recv_to, group, panel):
         pltpu.make_async_remote_copy(
-            src_ref=packed.at[group],
-            dst_ref=received.at[stop, my_group],
-            send_sem=send_sem,
-            recv_sem=recv_sems.at[stop],
-            device_id=peer,
-            device_id_type=MESH,
+            src_ref=src, dst_ref=dst, send_sem=send_to, recv_sem=recv_to,
+            device_id={"acq": group, "rcv": panel}, device_id_type=MESH,
         ).start()
-    received[back_reach, my_group] = packed[my_group]
+
+    if relayed:
+        @pl.when(my_panel == 0)
+        def _():
+            pl.semaphore_wait(barrier, groups)
+            send(packed, relay, send_sem, relay_sems.at[0], my_group, relay_panel)
+
+        @pl.when(my_panel == relay_panel)
+        def _():
+            pl.semaphore_wait(barrier, 3 * groups - 1)
+
+        @pl.when((my_panel == last) | ((my_panel > 0) & (my_panel < relay_panel)))
+        def _():
+            pl.semaphore_wait(barrier, 2 * groups - 1)
+
+        @pl.when(my_panel > 0)
+        def _():
+            for step in range(groups):
+                group = moved(my_group, step, groups)
+                send(
+                    packed.at[group], received.at[1, my_group], send_sem, recv_sems.at[1],
+                    group, my_panel - 1,
+                )
+
+        for step in range(1, groups):
+            group = moved(my_group, step, groups)
+            send(
+                packed.at[group], received.at[0, my_group], send_sem, recv_sems.at[0],
+                group, my_panel,
+            )
+
+        @pl.when(my_panel == relay_panel)
+        def _():
+            pltpu.make_async_copy(relay, relay, relay_sems.at[0]).wait()
+            for step in range(groups):
+                group = moved(my_group, step, groups)
+                send(
+                    relay.at[group], received.at[1, my_group], relay_sems.at[1], recv_sems.at[1],
+                    group, last,
+                )
+
+        received[back_reach, my_group] = packed[my_group]
+        pl.when(jnp.logical_not(waits_long))(prepare)
+    else:
+        pl.semaphore_wait(barrier, groups * stops - 1)
+        for stop, group, peer in peers(-1):
+            send(
+                packed.at[group], received.at[stop, my_group], send_sem, recv_sems.at[stop],
+                group, peer["rcv"],
+            )
+        received[back_reach, my_group] = packed[my_group]
+        prepare()
 
     totals = [jnp.zeros((pairs, width), F32)] * freq_count
     for stop in reversed(far_first):
@@ -192,7 +264,7 @@
         for group in range(groups):
             slots[stop, group * tile:group * tile + rows] = received[stop, group].astype(F32)
         regular = jnp.dot(
-            mixers, slots[stop].astype(BF16), preferred_element_type=F32
+            mixers[...], slots[stop].astype(BF16), preferred_element_type=F32
         ).astype(BF16)
         for f in range(freq_count):
             at = 2 * f * pairs
@@ -211,6 +283,10 @@
         if stop == back_reach:
             sent = packed.at[pl.ds(0, groups - 1)]
         pltpu.make_async_copy(sent, sent, send_sem).wait()
+    if relayed:
+        @pl.when(my_panel == relay_panel)
+        def _():
+            pltpu.make_async_copy(relay, relay, relay_sems.at[1]).wait()
 
 
 def shards(raw_blocks, raw_dest, raw_count, stencil, stencil_weight, kern):
@@ -241,12 +317,15 @@
             pltpu.VMEM(kern.shape, BF16),
             pltpu.VMEM((groups, rows, width), BF16),
             pltpu.VMEM((stops, groups, rows, width), BF16),
+            pltpu.VMEM((groups, rows, width), BF16),
             pltpu.VMEM((stops, groups * tile, width), F32),
+            pltpu.VMEM((2 * freq_count * 2 * shot_count, groups * tile), BF16),
             pltpu.VMEM((freq_count, 2 * stops * width, width), BF16),
             pltpu.SemaphoreType.DMA((raw_slots, 2)),
             pltpu.SemaphoreType.DMA((5,)),
             pltpu.SemaphoreType.DMA,
             pltpu.SemaphoreType.DMA((stops,)),
+            pltpu.SemaphoreType.DMA((2,)),
         ],
         compiler_params=pltpu.CompilerParams(
             collective_id=0, has_side_effects=True, vmem_limit_bytes=32 * 1024 * 1024

time: 11.3 us -> 10.7 us (0.947)
  the two profiles are of different devices: /device:TPU:0 before, /device:TPU:25 now
where the time goes in v6:
time: 10.7 us; the launch traced here: 10.6 us
  Pallas kernels  9.26 us (87%)
  between operations  0.66 us (6%)
  local copies, waits for them, and re-layouts  0.63 us (6%)
    pallas_call x1, Pallas kernels, shards(): pl.pallas_call(functools.partial(kernel, groups, panels, stops), out_shap...  9.26 us
    unnamed x1, local copies, waits for them, and re-layouts  0.63 us

profile of v6, /device:TPU:25, one launch (start us, length us, event | category | flops | bytes accessed | tf_op | source)
XLA Modules:
  0.0 10.6 jit_solution(14813508107805515207)
XLA Ops:
  0.7 9.3 %shard_map.73 = bf16[2,128,128]{2,1,0:T(8,128)(2,1)S(1)} custom-call(bf16[16,1024]{1,0:T(8,128)(2,1)} %constant.2.clone.table_hbm, bf16[4,1024,128]{2,1,0:T(8,128)(2,1)} %raw_hbm.1, s32[4]{0:T(128)} %dest_hbm.1, s32[1]{0:T(128)S(6)} %copy.11.count_ref, s32[2,64]{1,0:T(2,128)} %bitcast.6, bf16[2,64]{1,0:T(2,128)(2,1)} %bitcast.7, bf16[2,2,384]{2,1,0:T(2,128)(2,1)} %kern_hbm.1), custom_call_target="tpu_custom_call" | custom-call | tf_op jit(solution)/shard_map/pallas_call | solution.py:303
  9.9 0.6 %copy.10 = bf16[2,64,1,2,128]{4,3,2,1,0:T(2,128)(2,1)} copy(bf16[2,64,1,2,128]{4,3,2,1,0:T(2,128)(2,1)S(1)} %bitcast.5) | data formatting | bytes 131072

commit v7 on v6

--- a/solution.py
+++ b/solution.py
@@ -75,15 +75,29 @@
             return jnp.where(place < 0, place + count, place)
         return jnp.where(place >= count, place - count, place)
 
+    if groups & (groups - 1):
+        everyone = [moved(my_group, step, groups) for step in range(groups)]
+    else:
+        bits = range(groups.bit_length() - 1)
+        flips = [(1 << bit) - (2 << bit) * (my_group // (1 << bit) % 2) for bit in bits]
+        everyone = []
+        for mask in sorted(range(groups), key=lambda mask: (-bin(mask >> 1).count("1"), -mask)):
+            group = my_group
+            for bit in bits:
+                if mask >> bit & 1:
+                    group = group + flips[bit]
+            everyone.append(group)
+        everyone = everyone[-1:] + everyone[:-1]
+    others = everyone[1:]
+    everyone = everyone[1:] + everyone[:1]
+
     far_first = sorted(range(stops), key=lambda stop: -abs(stop - back_reach))
 
     def peers(sign):
         for stop in far_first:
             panel = moved(my_panel, sign * (stop - back_reach), panels)
-            for step in range(groups):
-                if stop != back_reach or step != 0:
-                    group = moved(my_group, step, groups)
-                    yield stop, group, {"acq": group, "rcv": panel}
+            for group in others if stop == back_reach else everyone:
+                yield stop, group, {"acq": group, "rcv": panel}
 
     relayed = stops == 2 and panels >= 4
     last = panels - 1
@@ -101,10 +115,10 @@
             greet(my_group, 0)
 
         sender_panel = jnp.where(my_panel == last, relay_panel, my_panel + 1)
-        for step in range(groups):
-            greet(moved(my_group, step, groups), sender_panel)
-        for step in range(1, groups):
-            greet(moved(my_group, step, groups), my_panel)
+        for group in everyone:
+            greet(group, sender_panel)
+        for group in others:
+            greet(group, my_panel)
     else:
         for _, group, peer in peers(1):
             greet(group, peer["rcv"])
@@ -219,15 +233,13 @@
 
         @pl.when(my_panel > 0)
         def _():
-            for step in range(groups):
-                group = moved(my_group, step, groups)
+            for group in everyone:
                 send(
                     packed.at[group], received.at[1, my_group], send_sem, recv_sems.at[1],
                     group, my_panel - 1,
                 )
 
-        for step in range(1, groups):
-            group = moved(my_group, step, groups)
+        for group in others:
             send(
                 packed.at[group], received.at[0, my_group], send_sem, recv_sems.at[0],
                 group, my_panel,
@@ -236,8 +248,7 @@
         @pl.when(my_panel == relay_panel)
         def _():
             pltpu.make_async_copy(relay, relay, relay_sems.at[0]).wait()
-            for step in range(groups):
-                group = moved(my_group, step, groups)
+            for group in everyone:
                 send(
                     relay.at[group], received.at[1, my_group], relay_sems.at[1], recv_sems.at[1],
                     group, last,

time: 10.7 us -> 10.4 us (0.972)
  the two profiles are of different devices: /device:TPU:25 before, /device:TPU:0 now
where the time goes in v7:
time: 10.4 us; the launch traced here: 10.3 us
  Pallas kernels  8.98 us (86%)
  between operations  0.66 us (6%)
  local copies, waits for them, and re-layouts  0.63 us (6%)
    pallas_call x1, Pallas kernels, shards(): pl.pallas_call(functools.partial(kernel, groups, panels, stops), out_shap...  8.98 us
    unnamed x1, local copies, waits for them, and re-layouts  0.63 us

profile of v7, /device:TPU:0, one launch (start us, length us, event | category | flops | bytes accessed | tf_op | source)
XLA Modules:
  0.0 10.3 jit_solution(18243835474965725543)
XLA Ops:
  0.7 9.0 %shard_map.73 = bf16[2,128,128]{2,1,0:T(8,128)(2,1)S(1)} custom-call(bf16[16,1024]{1,0:T(8,128)(2,1)} %constant.2.clone.table_hbm, bf16[4,1024,128]{2,1,0:T(8,128)(2,1)} %raw_hbm.1, s32[4]{0:T(128)} %dest_hbm.1, s32[1]{0:T(128)S(6)} %copy.11.count_ref, s32[2,64]{1,0:T(2,128)} %bitcast.6, bf16[2,64]{1,0:T(2,128)(2,1)} %bitcast.7, bf16[2,2,384]{2,1,0:T(2,128)(2,1)} %kern_hbm.1), custom_call_target="tpu_custom_call" | custom-call | tf_op jit(solution)/shard_map/pallas_call | solution.py:314
  9.6 0.6 %copy.10 = bf16[2,64,1,2,128]{4,3,2,1,0:T(2,128)(2,1)} copy(bf16[2,64,1,2,128]{4,3,2,1,0:T(2,128)(2,1)S(1)} %bitcast.5) | data formatting | bytes 131072

commit v8 on v7

--- a/solution.py
+++ b/solution.py
@@ -114,6 +114,11 @@
         def _():
             greet(my_group, 0)
 
+    for block in loads:
+        for load in block:
+            load.start()
+
+    if relayed:
         sender_panel = jnp.where(my_panel == last, relay_panel, my_panel + 1)
         for group in everyone:
             greet(group, sender_panel)
@@ -122,9 +127,6 @@
     else:
         for _, group, peer in peers(1):
             greet(group, peer["rcv"])
-    for block in loads:
-        for load in block:
-            load.start()
     for copy in small:
         copy.start()
     slots[...] = jnp.zeros_like(slots)

time: 10.4 us -> 10.4 us (level)
  the two profiles are of different devices: /device:TPU:0 before, /device:TPU:24 now
where the time goes in v8:
time: 10.4 us; the launch traced here: 10.3 us
  Pallas kernels  8.99 us (86%)
  between operations  0.66 us (6%)
  local copies, waits for them, and re-layouts  0.63 us (6%)
    pallas_call x1, Pallas kernels, shards(): pl.pallas_call(functools.partial(kernel, groups, panels, stops), out_shap...  8.99 us
    unnamed x1, local copies, waits for them, and re-layouts  0.63 us

profile of v8, /device:TPU:24, one launch (start us, length us, event | category | flops | bytes accessed | tf_op | source)
XLA Modules:
  0.0 10.3 jit_solution(894131294556536786)
XLA Ops:
  0.7 9.0 %shard_map.73 = bf16[2,128,128]{2,1,0:T(8,128)(2,1)S(1)} custom-call(bf16[16,1024]{1,0:T(8,128)(2,1)} %constant.2.clone.table_hbm, bf16[4,1024,128]{2,1,0:T(8,128)(2,1)} %raw_hbm.1, s32[4]{0:T(128)} %dest_hbm.1, s32[1]{0:T(128)S(6)} %copy.11.count_ref, s32[2,64]{1,0:T(2,128)} %bitcast.6, bf16[2,64]{1,0:T(2,128)(2,1)} %bitcast.7, bf16[2,2,384]{2,1,0:T(2,128)(2,1)} %kern_hbm.1), custom_call_target="tpu_custom_call" | custom-call | tf_op jit(solution)/shard_map/pallas_call | solution.py:316
  9.6 0.6 %copy.10 = bf16[2,64,1,2,128]{4,3,2,1,0:T(2,128)(2,1)} copy(bf16[2,64,1,2,128]{4,3,2,1,0:T(2,128)(2,1)S(1)} %bitcast.5) | data formatting | bytes 131072

commit v9 on v8

--- a/solution.py
+++ b/solution.py
@@ -334,7 +334,7 @@
             pltpu.VMEM((stops, groups * tile, width), F32),
             pltpu.VMEM((2 * freq_count * 2 * shot_count, groups * tile), BF16),
             pltpu.VMEM((freq_count, 2 * stops * width, width), BF16),
-            pltpu.SemaphoreType.DMA((raw_slots, 2)),
+            pltpu.SemaphoreType.DMA((raw_slots, 1)),
             pltpu.SemaphoreType.DMA((5,)),
             pltpu.SemaphoreType.DMA,
             pltpu.SemaphoreType.DMA((stops,)),

time: 10.4 us -> 10.4 us (level)
  no operation moved by 1% of the time
where the time goes in v9:
time: 10.4 us; the launch traced here: 10.2 us
  Pallas kernels  8.95 us (86%)
  between operations  0.66 us (6%)
  local copies, waits for them, and re-layouts  0.63 us (6%)
    pallas_call x1, Pallas kernels, shards(): pl.pallas_call(functools.partial(kernel, groups, panels, stops), out_shap...  8.95 us
    unnamed x1, local copies, waits for them, and re-layouts  0.63 us

profile of v9, /device:TPU:24, one launch (start us, length us, event | category | flops | bytes accessed | tf_op | source)
XLA Modules:
  0.0 10.2 jit_solution(7551535937555978338)
XLA Ops:
  0.7 9.0 %shard_map.73 = bf16[2,128,128]{2,1,0:T(8,128)(2,1)S(1)} custom-call(bf16[16,1024]{1,0:T(8,128)(2,1)} %constant.2.clone.table_hbm, bf16[4,1024,128]{2,1,0:T(8,128)(2,1)} %raw_hbm.1, s32[4]{0:T(128)} %dest_hbm.1, s32[1]{0:T(128)S(6)} %copy.11.count_ref, s32[2,64]{1,0:T(2,128)} %bitcast.6, bf16[2,64]{1,0:T(2,128)(2,1)} %bitcast.7, bf16[2,2,384]{2,1,0:T(2,128)(2,1)} %kern_hbm.1), custom_call_target="tpu_custom_call" | custom-call | tf_op jit(solution)/shard_map/pallas_call | solution.py:316
  9.6 0.6 %copy.10 = bf16[2,64,1,2,128]{4,3,2,1,0:T(2,128)(2,1)} copy(bf16[2,64,1,2,128]{4,3,2,1,0:T(2,128)(2,1)S(1)} %bitcast.5) | data formatting | bytes 131072
